TPU v7x, 256 devices: a whole 4x4x8 slice. The times are simulated.
256 devices in a mesh: row: 32 (over z_hi, x, y), col: 8 (over z_lo, core).
Axes of the slice: x: 4, y: 4, z: 8 (z_hi: 2, z_lo: 4; z = z_hi * 4 + z_lo), core: 2. Of those that a mesh axis runs over, the one named last changes fastest.
Arguments:
- out_grads: bfloat16 [2048, 13824], P(None, 'col'), may hold values from -6 to 6
- inputs: bfloat16 [2048, 5120], P(None, 'row'), may hold values from -6 to 6
- out_basis: bfloat16 [13824, 13824], P('col', 'row'), may hold values from -0.0546875 to 0.0546875
- in_basis: bfloat16 [5120, 5120], P('row', 'col'), may hold values from -0.078125 to 0.078125
Outputs:
- correction: float32 [13824, 5120], P('row', 'col')
All inputs are finite; a program needn't handle non-finite values.
Results may differ from a plain program's by a relative error of at most 0.0041.
Values may be sent and summed in bfloat16 or wider, within the bound.
A program may use at most 64 MiB of HBM per device.

v0:
```python
import jax
import jax.numpy as jnp
from jax import lax
from jax.sharding import PartitionSpec as P

SEQS = 2


def on_device(out_grads, inputs, out_basis, in_basis):
    total_rows = out_grads.shape[0]
    out_share = lax.psum_scatter(
        jnp.dot(out_grads, out_basis, preferred_element_type=jnp.float32),
        "col",
        scatter_dimension=0,
        tiled=True,
    ).astype(jnp.bfloat16)
    out_rotated = lax.all_gather(out_share, "col", axis=0, tiled=True)
    partial_in = jnp.dot(inputs, in_basis, preferred_element_type=jnp.float32)
    in_rotated = lax.psum(partial_in, "row").astype(jnp.bfloat16)
    seq_len = total_rows // SEQS
    out_seqs = out_rotated.reshape(SEQS, seq_len, out_rotated.shape[1])
    in_seqs = in_rotated.reshape(SEQS, seq_len, in_rotated.shape[1])
    products = lax.dot_general(
        out_seqs, in_seqs, (((1,), (1,)), ((0,), (0,))), preferred_element_type=jnp.float32
    )
    return jnp.sum(products * products, axis=0) / jnp.float32(total_rows)


def solution(mesh):
    in_specs = (P(None, "col"), P(None, "row"), P("col", "row"), P("row", "col"))
    out_specs = P("row", "col")
    return jax.shard_map(
        on_device, mesh=mesh, in_specs=in_specs, out_specs=out_specs, check_vma=False
    )
```

profile of v0, /device:TPU:1, one launch (start us, length us, event | category | flops | bytes accessed | tf_op | source)
XLA Modules:
  0.0 378.7 jit_solution(6832716797134892888)
XLA Ops:
  6.5 0.0 copy-start
  6.5 0.0 reduce-scatter.2.cloned.1.call-start
  6.5 1.4 copy-done
  7.9 8.2 %fusion.3 = f32[2048,432]{0,1:T(8,128)} fusion(bf16[1728,432]{0,1:T(8,128)(2,1)S(1)} %copy-done, bf16[2048,1728]{0,1:T(8,128)(2,1)} %param.4), kind=kOutput, calls=%fused_computation.5 | convolution fusion | flops 3057647616 | bytes 12109824 | tf_op jit(solution)/shard_map/dot_general | solution.py:12
  16.1 0.0 copy-start.1
  16.1 0.0 copy-start.2
  16.1 0.0 reduce-scatter.2.cloned.1.call-update
  16.1 0.0 all-gather.2.cloned.1.call-start
  16.2 1.0 copy-done.1
  17.2 0.0 copy-done.2
  17.2 3.3 fusion.2
  20.6 46.2 %reduce-scatter.2.cloned.1.call-done = f32[256,432]{0,1:T(8,128)} async-done(((f32[2048,432]{0,1:T(8,128)}), f32[256,432]{0,1:T(8,128)}) %reduce-scatter.2.cloned.1.call-update) | async-done | bytes 442384 | tf_op jit(solution)/shard_map/reduce_scatter | solution.py:11
  66.8 1.7 convert_element_type.6
  68.5 0.0 all-gather.2.cloned.1.call-update
  68.5 298.4 %all-reduce.1 = bf16[2048,640]{1,0:T(8,128)(2,1)} all-reduce(f32[2048,640]{1,0:T(8,128)} %fusion.2), channel_id=1, replica_groups=mesh['row'=32,'col'=8] {'row'}, use_global_device_ids=true, to_apply=%region_1.0 | all-reduce | flops 1310720 | bytes 7864320 | tf_op jit(solution)/shard_map/psum | solution.py:19
  366.9 0.0 all-gather.2.cloned.1.call-done
  366.9 3.9 %multiply_reduce_fusion = f32[432,640]{1,0:T(8,128)S(1)} fusion(bf16[2,1024,640]{2,1,0:T(8,128)(2,1)} %bitcast.10, bf16[54,2,8,1024]{3,2,1,0:T(8,128)(2,1)} %bitcast.11), kind=kOutput, calls=%fused_computation | convolution fusion | flops 1133291520 | bytes 5496832 | tf_op jit(solution)/shard_map/dot_general | solution.py:23
  370.8 1.1 broadcast_multiply_fusion
Async XLA Ops:
  6.5 1.4 copy-start
  6.5 60.2 %reduce-scatter.2.cloned.1.call-start = ((), (), s32[]{:S(2)}) async-start(), calls=%async_computation.1 | async-start | bytes 3981312 | tf_op jit(solution)/shard_map/reduce_scatter | solution.py:11
  16.1 1.1 copy-start.1
  16.1 1.1 copy-start.2
  16.1 350.8 %all-gather.2.cloned.1.call-start = ((), (), s32[]{:S(2)}) async-start(), calls=%async_computation.2 | async-start | bytes 1990656 | tf_op jit(solution)/shard_map/all_gather | solution.py:17
Sparse Core Ops, SparseCore 0:
  16.3 50.4 reduce-scatter.1
  68.6 65.7 all-gather.1
where the time goes:
time: 385 us; the launch traced here: 379 us
  blocking collectives  298 us (77%)
  waiting for transfers between devices  46.2 us (12%)
  matrix products  15.4 us (4%)
  between operations  13.4 us (3%)
    psum x1, blocking collectives, on_device(): in_rotated = lax.psum(partial_in, 'row').astype(jnp.bfloat16)  298 us
    reduce_scatter x1, waiting for transfers between devices, on_device(): lax.psum_scatter(jnp.dot(out_grads, out_basis, preferred_element_type=jnp...  46.2 us
    dot_general x1, matrix products, on_device(): jnp.dot(out_grads, out_basis, preferred_element_type=jnp.float32)  8.17 us
  transfers between devices with their start and end apart: 2, of which 1 were waited for; matrix products, arithmetic and copies ran while one was open for 1% of the time, Pallas kernels for 0%

commit v1 on v0

v1 whole, which is shorter than its diff:
```python
import jax
import jax.numpy as jnp
from jax import lax
from jax.experimental import pallas as pl
from jax.experimental.pallas import tpu as pltpu
from jax.sharding import PartitionSpec as P

MESH = pl.DeviceIdType.MESH
F32 = jnp.float32
BF16 = jnp.bfloat16

ROWS = 2048
SEQ = 1024
KO = 1728
DO = 432
KI = 160
DI = 640
WP = 384
WQ = DI - WP
NC = 8
TC = SEQ // NC
NS = 2
TS = 512 // NS
TO = TS // 4
PEERS = (1, 3, 2)
RS = BF16


def kernel(
    og_hbm, inp_hbm, ob_hbm, ib_hbm, out_ref,
    og, inp, ob, obt, po, pi, ssum, sbuf, ra, rb, orot,
    xt0, xp, xq, bp, bq, fp, fq, sp, sq, rp, rq, gz, zs, zr, irp, irq,
    ld, og_sem, core_s, core_r, coreo_s, coreo_r, za_s, za_r, zb_s, zb_r, zc_s, zc_r,
    a_s, a_r, b_s, b_r, h_s, h_r, c1_s, c1_r, c2_s, c2_r,
):
    row = lax.axis_index("row")
    col = lax.axis_index("col")
    zh = row // 16
    x = (row // 4) % 4
    y = row % 4
    zl = col // 2
    core = col % 2
    pu = y * (1 - core) + x * core
    pv = x * (1 - core) + y * core

    def uv(du, dv):
        dy = du * (1 - core) + dv * core
        dx = dv * (1 - core) + du * core
        return (zh * 16 + ((x + dx) % 4) * 4 + (y + dy) % 4, col)

    other_core = (row, zl * 2 + 1 - core)
    partner = ((1 - zh) * 16 + x * 4 + y, col)

    def remote(src, dst, s, r, dev):
        return pltpu.make_async_remote_copy(
            src_ref=src, dst_ref=dst, send_sem=s, recv_sem=r, device_id=dev, device_id_type=MESH
        )

    ld_inp = pltpu.make_async_copy(inp_hbm, inp, ld.at[0])
    ld_bp = pltpu.make_async_copy(ib_hbm.at[:, 0:WP], bp.at[pl.ds(pl.multiple_of(pu * KI, 32), KI)], ld.at[1])
    ld_bq = pltpu.make_async_copy(ib_hbm.at[:, WP:DI], bq.at[pl.ds(pl.multiple_of(pv * KI, 32), KI)], ld.at[2])
    ld_ob = pltpu.make_async_copy(ob_hbm, ob, ld.at[3])
    for c in (ld_inp, ld_bp, ld_bq, ld_ob):
        c.start()
    mine = pl.multiple_of(core * SEQ, SEQ)
    theirs = pl.multiple_of((1 - core) * SEQ, SEQ)
    og_loads = []
    for jj in range(4):
        for k, base in enumerate((theirs, mine)):
            rows = pl.ds(pl.multiple_of(base + jj * 256, 256), 256)
            c = pltpu.make_async_copy(og_hbm.at[rows], og.at[rows], og_sem.at[jj, k])
            c.start()
            og_loads.append(c)

    barrier = pltpu.get_barrier_semaphore()

    def greet(dev):
        pl.semaphore_signal(barrier, inc=1, device_id=dev, device_id_type=MESH)

    for d in PEERS:
        greet(uv(d, 0))
        greet(uv(0, d))
    greet(other_core)
    greet(partner)

    @pl.when(zl > 0)
    def _():
        greet((row, col - 2))

    @pl.when(zl < 3)
    def _():
        greet((row, col + 2))

    ends = jnp.where((zl == 0) | (zl == 3), 1, 0)
    sends = []

    ld_inp.wait()
    for k in range(4):
        xt0[:, k * 512:(k + 1) * 512] = inp[k * 512:(k + 1) * 512, :].T
    xp[pl.ds(pl.multiple_of(pu * KI, 32), KI), :] = xt0[:, pl.ds(pl.multiple_of(pu * 512, 512), 512)]
    xq[pl.ds(pl.multiple_of(pv * KI, 32), KI), :] = xt0[:, pl.ds(pl.multiple_of(pv * 512, 512), 512)]
    ld_bp.wait()
    ld_bq.wait()

    pl.semaphore_wait(barrier, 10 - ends)

    a_copies = []
    for i, d in enumerate(PEERS):
        for g, (pos, dev, xb, bb) in enumerate(((pu, uv(d, 0), xp, bp), (pv, uv(0, d), xq, bq))):
            own = pl.ds(pl.multiple_of(pos * KI, 32), KI)
            to = pl.ds(pl.multiple_of(((pos + d) % 4) * 512, 512), 512)
            c = remote(bb.at[own], bb.at[own], a_s.at[0, g, i], a_r.at[0, g, i], dev)
            c.start()
            a_copies.append(c)
            c = remote(xt0.at[:, to], xb.at[own], a_s.at[1, g, i], a_r.at[1, g, i], dev)
            c.start()
            a_copies.append(c)
    sends += a_copies

    ld_ob.wait()
    obt[...] = ob[...].T

    def out_product(base, jj, k):
        og_loads[jj * 2 + k].wait()
        g = og[pl.ds(pl.multiple_of(base + jj * 256, 256), 256), :]
        return lax.dot_general(obt[...], g, (((1,), (1,)), ((), ())), preferred_element_type=F32)

    core_copies = []

    def out_theirs(jj):
        po[jj] = out_product(theirs, jj, 0)
        c = remote(po.at[jj], pi.at[jj], core_s.at[jj], core_r.at[jj], other_core)
        c.start()
        core_copies.append(c)
        sends.append(c)

    def role(j):
        return zl if j % 2 == 0 else 3 - zl

    def step(j, by):
        return (row, col + 2 * by if j % 2 == 0 else col - 2 * by)

    def za(j, by):
        return remote(sbuf.at[j], ra.at[j], za_s.at[j], za_r.at[j], step(j, by))

    def zb(j):
        return remote(sbuf.at[j], rb.at[j], zb_s.at[j], zb_r.at[j], step(j, -1))

    def tokens(j):
        return pl.ds(pl.multiple_of(mine + j * TC, TC), TC)

    def zc(j, by, k):
        at = orot.at[:, tokens(j)]
        return remote(at, at, zc_s.at[j, k], zc_r.at[j], step(j, by))

    def co(j):
        at = orot.at[:, tokens(j)]
        return remote(at, at, coreo_s.at[j], coreo_r.at[j], other_core)

    def out_mine(jj):
        own = out_product(mine, jj, 1)
        core_copies[jj].wait_recv()
        total = own + pi[jj]
        for h in range(2):
            j = 2 * jj + h
            part = total[:, h * TC:(h + 1) * TC]
            ssum[j] = part
            p = role(j)

            @pl.when(p == 0)
            def _():
                sbuf[j] = part.astype(BF16)
                za(j, 1).start()

            @pl.when(p == 3)
            def _():
                sbuf[j] = part.astype(BF16)
                za(j, -1).start()

    def out_a(j):
        @pl.when(role(j) == 2)
        def _():
            za(j, 1).wait_recv()
            sbuf[j] = (ssum[j] + ra[j].astype(F32)).astype(BF16)
            zb(j).start()

    def out_b(j):
        @pl.when(role(j) == 1)
        def _():
            za(j, 1).wait_recv()
            zb(j).wait_recv()
            orot[:, tokens(j)] = (ssum[j] + ra[j].astype(F32) + rb[j].astype(F32)).astype(BF16)
            zc(j, -1, 0).start()
            zc(j, 1, 1).start()
            co(j).start()

    def out_c(j):
        @pl.when(role(j) == 2)
        def _():
            zc(j, 1, 0).wait_recv()
            zc(j, 1, 0).start()
            co(j).start()

    def out_d(j):
        p = role(j)

        @pl.when((p == 0) | (p == 3))
        def _():
            zc(j, 1, 0).wait_recv()
            co(j).start()

    def out_end(j):
        co(j).wait_recv()
        co(j).wait_send()
        p = role(j)

        @pl.when(p == 0)
        def _():
            za(j, 1).wait_send()

        @pl.when(p == 3)
        def _():
            za(j, -1).wait_send()

        @pl.when(p == 2)
        def _():
            zb(j).wait_send()
            zc(j, 1, 0).wait_send()

        @pl.when(p == 1)
        def _():
            zc(j, -1, 0).wait_send()
            zc(j, 1, 1).wait_send()

    blocks = ((0, pv, lambda d: uv(0, d), xp, bp, fp, sp, rp), (1, pu, lambda d: uv(d, 0), xq, bq, fq, sq, rq))
    b_copies = {}

    def in_partial(st):
        for g, pos, dev, xb, bb, f, s, r in blocks:
            part = jnp.dot(xb[:, st * TS:(st + 1) * TS].T, bb[...], preferred_element_type=F32)
            f[st] = part
            s[st] = part.astype(RS)
            for i, d in enumerate(PEERS):
                to = pl.ds(pl.multiple_of(((pos + d) % 4) * TO, TO), TO)
                c = remote(s.at[st, to], r.at[st, i], b_s.at[st, g, i], b_r.at[st, g, i], dev(d))
                c.start()
                b_copies[st, g, i] = c
                sends.append(c)

    h_copies = {}

    def in_cross(st):
        for g, pos, dev, xb, bb, f, s, r in blocks:
            for i in range(3):
                b_copies[st, g, i].wait_recv()
            total = f[st, pl.ds(pl.multiple_of(pos * TO, TO), TO), :]
            for i in range(3):
                total = total + r[st, i].astype(F32)
            lanes = slice(0, WP) if g == 0 else slice(WP, DI)
            gz[st, :, lanes] = total
            zs[st, :, lanes] = total.astype(BF16)
        c = remote(zs.at[st], zr.at[st], h_s.at[st], h_r.at[st], partner)
        c.start()
        h_copies[st] = c
        sends.append(c)

    gather = (
        (0, irp, pu, pv, lambda d: uv(d, 0), lambda d: uv(0, d)),
        (1, irq, pv, pu, lambda d: uv(0, d), lambda d: uv(d, 0)),
    )
    c2 = {}

    def sub(buf, first, second, st):
        return buf.at[pl.ds(pl.multiple_of(first * 512 + st * TS + second * TO, TO), TO)]

    def c2_send(st, g, k, side):
        _, buf, first, second, along, across = gather[g]
        at = sub(buf, first, (second + k) % 4, st)
        c = remote(at, at, c2_s.at[st, g, side, k], c2_r.at[st, g, side, k], along(1 if side == 0 else 3))
        c.start()
        c2[st, g, side, k] = c
        sends.append(c)

    c1 = {}

    def in_round(st):
        h_copies[st].wait_recv()
        for g, buf, first, second, along, across in gather:
            lanes = slice(0, WP) if g == 0 else slice(WP, DI)
            whole = gz[st, :, lanes] + zr[st, :, lanes].astype(F32)
            sub(buf, first, second, st)[...] = whole.astype(BF16)
        for g, buf, first, second, along, across in gather:
            at = sub(buf, first, second, st)
            for i, d in enumerate(PEERS):
                c = remote(at, at, c1_s.at[st, g, i], c1_r.at[st, g, i], across(d))
                c.start()
                c1[st, g, i] = c
                sends.append(c)
        for g in range(2):
            for side in range(2):
                c2_send(st, g, 0, side)

    def in_spread(st, i):
        k = (4 - PEERS[i]) % 4
        for g in range(2):
            c1[st, g, i].wait_recv()
            for side in range(2):
                c2_send(st, g, k, side)

    ORDER = (0, 3, 1, 2)
    c3 = {}

    def in_forward(st, side):
        for k in ORDER[:2] if side == 0 else ORDER[2:]:
            for g, buf, first, second, along, across in gather:
                c2[st, g, side, k].wait_recv()
                at = sub(buf, (first + (3 if side == 0 else 1)) % 4, (second + k) % 4, st)
                c = remote(at, at, c2_s.at[st, g, 2, k], c2_r.at[st, g, 2, k], along(1 if side == 0 else 3))
                c.start()
                c3[st, g, k] = c
                sends.append(c)

    def in_end(st):
        for g in range(2):
            for k in ORDER[2:]:
                c2[st, g, 0, k].wait_recv()
            for k in ORDER[:2]:
                c2[st, g, 1, k].wait_recv()
            for k in range(4):
                c3[st, g, k].wait_recv()

    for jj in range(4):
        out_theirs(jj)
        out_mine(jj)
    out_a(0)
    out_a(1)
    for c in a_copies:
        c.wait_recv()
    in_partial(0)
    in_partial(1)
    out_b(0)
    out_a(2)
    out_b(1)
    out_a(3)
    in_cross(0)
    out_c(0)
    out_b(2)
    out_a(4)
    in_cross(1)
    out_c(1)
    out_d(0)
    out_b(3)
    out_a(5)
    in_round(0)
    out_c(2)
    out_d(1)
    out_b(4)
    out_a(6)
    in_round(1)
    for i in range(3):
        in_spread(0, i)
    out_c(3)
    out_d(2)
    out_b(5)
    out_a(7)
    for i in range(3):
        in_spread(1, i)
    out_c(4)
    out_d(3)
    out_b(6)
    in_forward(0, 0)
    in_forward(0, 1)
    out_c(5)
    out_d(4)
    out_b(7)
    in_forward(1, 0)
    in_forward(1, 1)
    out_c(6)
    out_d(5)
    out_c(7)
    out_d(6)
    out_d(7)
    for j in range(NC):
        out_end(j)
    in_end(0)
    in_end(1)

    for m in range(3):
        rows = slice(m * 144, (m + 1) * 144)
        for lanes, ir in ((slice(0, WP), irp), (slice(WP, DI), irq)):
            acc = None
            for n in range(2):
                seq = slice(n * SEQ, (n + 1) * SEQ)
                prod = jnp.dot(orot[rows, seq], ir[seq, :], preferred_element_type=F32)
                acc = prod * prod if acc is None else acc + prod * prod
            out_ref[rows, lanes] = acc * F32(1.0 / ROWS)
    for c in sends:
        c.wait_send()


def on_device(out_grads, inputs, out_basis, in_basis):
    dma = pltpu.SemaphoreType.DMA
    vm = pltpu.VMEM
    return pl.pallas_call(
        kernel,
        out_shape=jax.ShapeDtypeStruct((DO, DI), F32),
        in_specs=[pl.BlockSpec(memory_space=pl.ANY)] * 4,
        out_specs=pl.BlockSpec(memory_space=pltpu.VMEM),
        scratch_shapes=[
            vm((ROWS, KO), BF16), vm((ROWS, KI), BF16), vm((KO, DO), BF16), vm((DO, KO), BF16),
            vm((4, DO, 256), F32), vm((4, DO, 256), F32), vm((NC, DO, TC), F32), vm((NC, DO, TC), BF16),
            vm((NC, DO, TC), BF16), vm((NC, DO, TC), BF16), vm((DO, ROWS), BF16),
            vm((KI, ROWS), BF16), vm((4 * KI, 512), BF16), vm((4 * KI, 512), BF16),
            vm((4 * KI, WP), BF16), vm((4 * KI, WQ), BF16),
            vm((NS, TS, WP), F32), vm((NS, TS, WQ), F32), vm((NS, TS, WP), RS), vm((NS, TS, WQ), RS),
            vm((NS, 3, TO, WP), RS), vm((NS, 3, TO, WQ), RS),
            vm((NS, TO, DI), F32), vm((NS, TO, DI), BF16), vm((NS, TO, DI), BF16),
            vm((ROWS, WP), BF16), vm((ROWS, WQ), BF16),
            dma((4,)), dma((4, 2)), dma((4,)), dma((4,)), dma((NC,)), dma((NC,)),
            dma((NC,)), dma((NC,)), dma((NC,)), dma((NC,)), dma((NC, 2)), dma((NC,)),
            dma((2, 2, 3)), dma((2, 2, 3)), dma((NS, 2, 3)), dma((NS, 2, 3)), dma((NS,)), dma((NS,)),
            dma((NS, 2, 3)), dma((NS, 2, 3)), dma((NS, 2, 3, 4)), dma((NS, 2, 3, 4)),
        ],
        compiler_params=pltpu.CompilerParams(
            collective_id=0, has_side_effects=True, vmem_limit_bytes=56 * 1024 * 1024
        ),
        cost_estimate=pl.CostEstimate(flops=4_600_000_000, bytes_accessed=10_600_000, transcendentals=0),
        name="correction",
    )(out_grads, inputs, out_basis, in_basis)


def solution(mesh):
    in_specs = (P(None, "col"), P(None, "row"), P("col", "row"), P("row", "col"))
    return jax.shard_map(
        on_device, mesh=mesh, in_specs=in_specs, out_specs=P("row", "col"), check_vma=False
    )
```

time: 385 us -> 83.9 us (0.22); the launches traced: 379 us -> 83.4 us
  blocking collectives: 298 us -> 0 us
  Pallas kernels: 0 us -> 66.5 us
  waiting for transfers between devices: 46.2 us -> 0 us
  matrix products: 15.4 us -> 0 us
  local copies, waits for them, and re-layouts: 2.45 us -> 16.9 us
  between operations: 13.4 us -> 0.01 us
    psum x1 -> x0, blocking collectives: 298 us -> none  [on_device(): in_rotated = lax.psum(partial_in, 'row').astype(jnp.bfloat16)]
    pallas_call x0 -> x1, Pallas kernels: none -> 66.5 us  [on_device(): pl.pallas_call(kernel, out_shape=jax.ShapeDtypeStruct((DO, DI), F32), in_...]
    reduce_scatter x1 -> x0, waiting for transfers between devices: 46.2 us -> none  [on_device(): lax.psum_scatter(jnp.dot(out_grads, out_basis, preferred_element_type=jnp...]
    dot_general x3 -> x0, matrix products: 15.4 us -> none  [the longest x1 8.17 us: on_device(): jnp.dot(out_grads, out_basis, preferred_element_type=jnp.float32)]
    unnamed x6, local copies, waits for them, and re-layouts: 2.45 us -> 16.9 us
  transfers between devices with their start and end apart: 2 -> 0, of which waited for: 1 -> 0; matrix products, arithmetic and copies ran while one was open for 1% -> 0% of each run, Pallas kernels for 0% -> 0%
where the time goes in v1:
time: 83.9 us; the launch traced here: 83.4 us
  Pallas kernels  66.5 us (79%)
  local copies, waits for them, and re-layouts  16.9 us (20%)
    pallas_call x1, Pallas kernels, on_device(): pl.pallas_call(kernel, out_shape=jax.ShapeDtypeStruct((DO, DI), F32), in_...  66.5 us
    unnamed x6, local copies, waits for them, and re-layouts  16.9 us

profile of v1, /device:TPU:1, one launch (start us, length us, event | category | flops | bytes accessed | tf_op | source)
XLA Modules:
  0.0 83.4 jit_solution(7830243911452819415)
XLA Ops:
  0.0 0.0 copy-start
  0.0 2.3 %copy.6.inp_hbm = bf16[2048,160]{1,0:T(8,128)(2,1)} copy(bf16[2048,160]{0,1:T(8,128)(2,1)} %param.5) | data formatting | bytes 1310720 | tf_op args[1]
  2.3 0.0 copy-done
  2.3 2.3 %copy.7.ob_hbm = bf16[1728,432]{1,0:T(8,128)(2,1)} copy(bf16[1728,432]{0,1:T(8,128)(2,1)S(1)} %copy-done) | data formatting | bytes 2985984 | tf_op args[2]
  4.6 10.0 %copy.5.og_hbm = bf16[2048,1728]{1,0:T(8,128)(2,1)} copy(bf16[2048,1728]{0,1:T(8,128)(2,1)} %param.4) | data formatting | bytes 14155776 | tf_op args[0]
  14.6 66.5 %correction.1 = f32[432,640]{1,0:T(8,128)} custom-call(bf16[2048,1728]{1,0:T(8,128)(2,1)} %copy.5.og_hbm, bf16[2048,160]{1,0:T(8,128)(2,1)} %copy.6.inp_hbm, bf16[1728,432]{1,0:T(8,128)(2,1)} %copy.7.ob_hbm, bf16[160,640]{1,0:T(8,128)(2,1)} %ib_hbm.1), custom_call_target="tpu_custom_call" | custom-call | flops 4600000000 | bytes 10600000 | tf_op jit(solution)/shard_map/correction/pallas_call | solution.py:404
  81.0 2.3 %copy.9 = f32[432,640]{1,0:T(8,128)} copy(f32[432,640]{1,0:T(8,128)} %correction.1) | data formatting | bytes 2211840
Async XLA Ops:
  0.0 2.3 %copy-start = (bf16[1728,432]{0,1:T(8,128)(2,1)S(1)}, bf16[1728,432]{0,1:T(8,128)(2,1)}, u32[]{:S(2)}) copy-start(bf16[1728,432]{0,1:T(8,128)(2,1)} %param.6) | copy-start | bytes 4478980

commit v2 on v1

v2 whole, which is shorter than its diff:
```python
import jax
import jax.numpy as jnp
from jax import lax
from jax.experimental import pallas as pl
from jax.experimental.pallas import tpu as pltpu
from jax.sharding import PartitionSpec as P

MESH = pl.DeviceIdType.MESH
F32 = jnp.float32
BF16 = jnp.bfloat16

ROWS = 2048
SEQ = 1024
KO = 1728
DO = 432
KI = 160
DI = 640
WP = 384
WQ = DI - WP
TC = 128
DH = 224
NC = 2 * SEQ // TC
NS = 4
TS = 512 // NS
TO = TS // 4
PEERS = (1, 3, 2)
HK = KI // 2
RS = BF16


def kernel(
    ogt_hbm, inpt_hbm, obt_hbm, ib_hbm, out_ref,
    og, obt, po, pi, ssum, sbuf, ra, rb, orot,
    xp, xq, bp, bq, fp, fq, sp, sq, rp, rq, gz, zs, zr, irp, irq,
    ld, og_sem, core_s, core_r, coreo_s, coreo_r, za_s, za_r, zb_s, zb_r, zc_s, zc_r,
    a_s, a_r, x_s, x_r, y_s, y_r, b_s, b_r, h_s, h_r, c1_s, c1_r, c2_s, c2_r, c3_s, c3_r,
):
    row = lax.axis_index("row")
    col = lax.axis_index("col")
    zh = row // 16
    x = (row // 4) % 4
    y = row % 4
    zl = col // 2
    core = col % 2
    pu = y * (1 - core) + x * core
    pv = x * (1 - core) + y * core

    def uv(du, dv):
        dy = du * (1 - core) + dv * core
        dx = dv * (1 - core) + du * core
        return (zh * 16 + ((x + dx) % 4) * 4 + (y + dy) % 4, col)

    other_core = (row, zl * 2 + 1 - core)
    partner = ((1 - zh) * 16 + x * 4 + y, col)

    def remote(src, dst, s, r, dev):
        return pltpu.make_async_remote_copy(
            src_ref=src, dst_ref=dst, send_sem=s, recv_sem=r, device_id=dev, device_id_type=MESH
        )

    def own_rows(pos):
        return pl.ds(pl.multiple_of(pos * HK, 16), HK)

    barrier = pltpu.get_barrier_semaphore()

    def greet(dev):
        pl.semaphore_signal(barrier, inc=1, device_id=dev, device_id_type=MESH)

    for d in PEERS:
        greet(uv(d, 0))
        greet(uv(0, d))
    greet(other_core)
    greet(partner)

    @pl.when(zl > 0)
    def _():
        greet((row, col - 2))

    @pl.when(zl < 3)
    def _():
        greet((row, col + 2))

    ends = jnp.where((zl == 0) | (zl == 3), 1, 0)
    sends = []

    pl.semaphore_wait(barrier, 10 - ends)

    half = pl.ds(pl.multiple_of(core * HK, 16), HK)
    axes = ((0, pu, lambda d: uv(d, 0), xp, xq, bp), (1, pv, lambda d: uv(0, d), xq, xp, bq))
    x_copies = {}
    b_blocks = []
    hand = {}

    def x_send(st):
        for i, d in enumerate(PEERS):
            for g, pos, dev, xb, _, _ in axes:
                to = pl.ds(pl.multiple_of(((pos + d) % 4) * 512 + st * TS, TS), TS)
                here = xb.at[core, own_rows(pos), pl.ds(st * TS, TS)]
                c = remote(inpt_hbm.at[half, to], here, x_s.at[st, g, i], x_r.at[st, g, i], dev(d))
                c.start()
                x_copies[st, g, i] = c
                sends.append(c)

    def x_hand(st):
        for g, pos, dev, xb, other, _ in axes:
            for i in range(3):
                x_copies[st, g, i].wait_recv()
            lanes = pl.ds(st * TS, TS)
            c = remote(xb.at[core, :, lanes], other.at[core, :, lanes], y_s.at[st, g], y_r.at[st, g], other_core)
            c.start()
            hand[st, g] = c
            sends.append(c)

    def basis_send():
        for i, d in enumerate(PEERS):
            for g, pos, dev, _, _, bb in axes:
                lanes = slice(0, WP) if g == 0 else slice(WP, DI)
                for h in range(2):
                    c = remote(
                        ib_hbm.at[h * HK:(h + 1) * HK, lanes], bb.at[h, own_rows(pos)],
                        a_s.at[g, i, h], a_r.at[g, i, h], dev(d),
                    )
                    c.start()
                    b_blocks.append(c)
                    sends.append(c)

    own_loads = []
    og_loads = {}
    ld_ob = pltpu.make_async_copy(obt_hbm, obt, ld.at[0])

    def load_own():
        for g, pos, _, xb, _, bb in axes:
            at = pl.ds(pl.multiple_of(pos * 512, 512), 512)
            lanes = slice(0, WP) if g == 0 else slice(WP, DI)
            own_loads.append(pltpu.make_async_copy(inpt_hbm.at[half, at], xb.at[core, own_rows(pos)], ld.at[1 + 3 * g]))
            for h in range(2):
                own_loads.append(
                    pltpu.make_async_copy(
                        ib_hbm.at[h * HK:(h + 1) * HK, lanes], bb.at[h, own_rows(pos)], ld.at[2 + 3 * g + h]
                    )
                )
        for c in own_loads:
            c.start()

    mine = pl.multiple_of(core * SEQ, SEQ)
    theirs = pl.multiple_of((1 - core) * SEQ, SEQ)

    def load_gradients(base, jj, k):
        at = pl.ds(pl.multiple_of(base + jj * 256, 256), 256)
        c = pltpu.make_async_copy(ogt_hbm.at[:, at], og.at[:, at], og_sem.at[jj, k])
        c.start()
        og_loads[jj, k] = c

    def out_product(base, jj, k):
        og_loads[jj, k].wait()
        g = og[:, pl.ds(pl.multiple_of(base + jj * 256, 256), 256)]
        return jnp.dot(obt[...], g, preferred_element_type=F32)

    core_copies = []

    def out_theirs(jj):
        po[jj] = out_product(theirs, jj, 0)
        c = remote(po.at[jj], pi.at[jj], core_s.at[jj], core_r.at[jj], other_core)
        c.start()
        core_copies.append(c)
        sends.append(c)

    def role(j):
        return zl if j % 2 == 0 else 3 - zl

    def step(j, by):
        return (row, col + 2 * by if j % 2 == 0 else col - 2 * by)

    def rows(j):
        return slice(0, DH) if j % 2 == 0 else slice(DH, DO)

    def za(j, by):
        return remote(
            sbuf.at[j // 2, rows(j)], ra.at[j // 2, rows(j)], za_s.at[j], za_r.at[j], step(j, by)
        )

    def zb(j):
        return remote(
            sbuf.at[j // 2, rows(j)], rb.at[j // 2, rows(j)], zb_s.at[j], zb_r.at[j], step(j, -1)
        )

    def piece(j):
        return orot.at[rows(j), pl.ds(pl.multiple_of(mine + (j // 2) * TC, TC), TC)]

    def zc(j, by, k):
        return remote(piece(j), piece(j), zc_s.at[j, k], zc_r.at[j], step(j, by))

    def co(j):
        return remote(piece(j), piece(j), coreo_s.at[j], coreo_r.at[j], other_core)

    def out_mine(jj):
        own = out_product(mine, jj, 1)
        core_copies[jj].wait_recv()
        total = own + pi[jj]
        for h in range(2):
            ssum[2 * jj + h] = total[:, h * TC:(h + 1) * TC]
            sbuf[2 * jj + h] = total[:, h * TC:(h + 1) * TC].astype(BF16)

    def out_send(j):
        p = role(j)

        @pl.when(p == 0)
        def _():
            za(j, 1).start()

        @pl.when(p == 3)
        def _():
            za(j, -1).start()

    def out_a(j):
        @pl.when(role(j) == 2)
        def _():
            za(j, 1).wait_recv()
            at = rows(j)
            sbuf[j // 2, at] = (ssum[j // 2, at] + ra[j // 2, at].astype(F32)).astype(BF16)
            zb(j).start()

    def out_b(j):
        @pl.when(role(j) == 1)
        def _():
            za(j, 1).wait_recv()
            zb(j).wait_recv()
            at = rows(j)
            total = ssum[j // 2, at] + ra[j // 2, at].astype(F32) + rb[j // 2, at].astype(F32)
            piece(j)[...] = total.astype(BF16)
            zc(j, 1, 1).start()
            zc(j, -1, 0).start()
            co(j).start()

    def out_c(j):
        @pl.when(role(j) == 2)
        def _():
            zc(j, 1, 0).wait_recv()
            zc(j, 1, 0).start()
            co(j).start()

    def out_d(j):
        p = role(j)

        @pl.when((p == 0) | (p == 3))
        def _():
            zc(j, 1, 0).wait_recv()
            co(j).start()

    def out_end(j):
        co(j).wait_recv()
        co(j).wait_send()
        p = role(j)

        @pl.when(p == 0)
        def _():
            za(j, 1).wait_send()

        @pl.when(p == 3)
        def _():
            za(j, -1).wait_send()

        @pl.when(p == 2)
        def _():
            zb(j).wait_send()
            zc(j, 1, 0).wait_send()

        @pl.when(p == 1)
        def _():
            zc(j, -1, 0).wait_send()
            zc(j, 1, 1).wait_send()

    blocks = ((0, pv, lambda d: uv(0, d), xp, bp, fp, sp, rp), (1, pu, lambda d: uv(d, 0), xq, bq, fq, sq, rq))
    b_copies = {}

    def in_partial(st):
        for g in range(2):
            hand[st, g].wait_recv()
        for g, pos, dev, xb, bb, f, s, r in blocks:
            turned = xb[:, :, st * TS:(st + 1) * TS].reshape(4 * KI, TS).T
            part = jnp.dot(turned, bb[...].reshape(4 * KI, bb.shape[-1]), preferred_element_type=F32)
            f[st] = part
            s[st] = part.astype(RS)
            for i, d in enumerate(PEERS):
                to = pl.ds(pl.multiple_of(((pos + d) % 4) * TO, TO), TO)
                c = remote(s.at[st, to], r.at[st, i], b_s.at[st, g, i], b_r.at[st, g, i], dev(d))
                c.start()
                b_copies[st, g, i] = c
                sends.append(c)

    h_copies = {}

    def in_cross(st):
        for g, pos, dev, xb, bb, f, s, r in blocks:
            for i in range(3):
                b_copies[st, g, i].wait_recv()
            total = f[st, pl.ds(pl.multiple_of(pos * TO, TO), TO), :]
            for i in range(3):
                total = total + r[st, i].astype(F32)
            lanes = slice(0, WP) if g == 0 else slice(WP, DI)
            gz[st, :, lanes] = total
            zs[st, :, lanes] = total.astype(BF16)
        c = remote(zs.at[st], zr.at[st], h_s.at[st], h_r.at[st], partner)
        c.start()
        h_copies[st] = c
        sends.append(c)

    gather = (
        (0, irp, pu, pv, lambda d: uv(d, 0), lambda d: uv(0, d)),
        (1, irq, pv, pu, lambda d: uv(0, d), lambda d: uv(d, 0)),
    )
    def sub(buf, first, second, st):
        return buf.at[pl.ds(pl.multiple_of(first * 512 + st * TS + second * TO, TO), TO)]

    c1 = {}

    def in_round(st):
        h_copies[st].wait_recv()
        for g, buf, first, second, along, across in gather:
            lanes = slice(0, WP) if g == 0 else slice(WP, DI)
            whole = gz[st, :, lanes] + zr[st, :, lanes].astype(F32)
            sub(buf, first, second, st)[...] = whole.astype(BF16)
        for g, buf, first, second, along, across in gather:
            at = sub(buf, first, second, st)
            for i, d in enumerate(PEERS):
                c = remote(at, at, c1_s.at[st, g, i], c1_r.at[st, g, i], across(d))
                c.start()
                c1[st, g, i] = c
                sends.append(c)

    c2 = {}
    c3 = {}

    def slab(buf, first, st, lo, n):
        return buf.at[pl.ds(pl.multiple_of(first * 512 + st * TS + lo, 16), n)]

    def in_spread(st):
        for g, buf, first, second, along, across in gather:
            for i in range(3):
                c1[st, g, i].wait_recv()
            at = slab(buf, first, st, 0, TS)
            for side in range(2):
                c = remote(at, at, c2_s.at[st, g, side], c2_r.at[st, g, side], along(1 + 2 * side))
                c.start()
                c2[st, g, side] = c
                sends.append(c)

    def in_forward(st):
        for side in range(2):
            for g, buf, first, second, along, across in gather:
                c2[st, g, side].wait_recv()
                at = slab(buf, (first + 3 - 2 * side) % 4, st, side * (TS // 2), TS // 2)
                c = remote(at, at, c3_s.at[st, g, side], c3_r.at[st, g, side], along(1 + 2 * side))
                c.start()
                c3[st, g, side] = c
                sends.append(c)

    def in_end(st):
        for g in range(2):
            for side in range(2):
                c3[st, g, side].wait_recv()

    x_send(0)
    x_send(1)
    basis_send()
    x_send(2)
    ld_ob.start()
    load_gradients(theirs, 0, 0)
    load_gradients(theirs, 1, 0)
    load_gradients(mine, 0, 1)
    load_own()
    for jj, k in ((2, 0), (1, 1), (3, 0), (2, 1), (3, 1)):
        load_gradients(mine if k else theirs, jj, k)
    ld_ob.wait()
    out_theirs(0)
    out_theirs(1)
    for c in own_loads:
        c.wait()
    x_hand(0)
    out_mine(0)
    out_send(0)
    out_send(1)
    out_send(2)
    out_send(3)
    out_mine(1)
    out_send(4)
    out_theirs(2)
    out_a(0)
    for c in b_blocks:
        c.wait_recv()
    in_partial(0)
    out_a(1)
    out_send(5)
    x_hand(1)
    out_mine(2)
    out_b(0)
    x_send(3)
    out_send(6)
    out_a(2)
    x_hand(2)
    out_b(1)
    out_send(7)
    out_a(3)
    in_partial(1)
    in_cross(0)
    out_send(8)
    out_a(4)
    in_partial(2)
    x_hand(3)
    out_c(0)
    out_b(2)
    out_c(1)
    in_cross(1)
    out_b(3)
    out_a(5)
    out_send(9)
    out_a(6)
    in_partial(3)
    out_c(2)
    out_a(7)
    out_b(4)
    in_cross(2)
    out_send(10)
    out_theirs(3)
    out_a(8)
    out_send(11)
    in_round(0)
    in_cross(3)
    out_b(5)
    out_c(3)
    out_mine(3)
    out_b(6)
    in_round(1)
    out_b(7)
    out_d(0)
    out_send(12)
    in_spread(0)
    out_a(9)
    out_a(10)
    out_b(8)
    out_d(1)
    in_round(2)
    in_spread(1)
    out_c(4)
    out_c(5)
    out_a(11)
    out_d(2)
    in_round(3)
    out_c(6)
    out_send(13)
    out_d(3)
    in_spread(2)
    out_send(14)
    out_send(15)
    out_c(7)
    in_forward(0)
    out_b(9)
    out_c(8)
    out_a(12)
    out_b(10)
    out_d(4)
    out_b(11)
    out_d(5)
    out_a(13)
    out_d(6)
    out_d(7)
    in_spread(3)
    out_c(9)
    out_a(14)
    out_c(10)
    out_a(15)
    in_forward(1)
    out_d(8)
    out_b(12)
    in_forward(2)
    out_c(11)
    out_b(13)
    in_forward(3)
    out_b(14)
    out_b(15)
    out_d(9)
    out_d(10)
    out_c(12)
    out_d(11)
    out_d(12)
    out_d(13)
    out_c(13)
    out_c(14)
    out_d(14)
    out_c(15)
    out_d(15)
    for j in range(NC):
        out_end(j)
    for st in range(NS):
        in_end(st)

    for m in range(3):
        part = slice(m * 144, (m + 1) * 144)
        for lanes, ir in ((slice(0, WP), irp), (slice(WP, DI), irq)):
            acc = None
            for n in range(2):
                seq = slice(n * SEQ, (n + 1) * SEQ)
                prod = jnp.dot(orot[part, seq], ir[seq, :], preferred_element_type=F32)
                acc = prod * prod if acc is None else acc + prod * prod
            out_ref[part, lanes] = acc * F32(1.0 / ROWS)
    for c in sends:
        c.wait_send()


def settle(src, dst, go):
    c = pltpu.make_async_copy(src, dst, go)
    c.start()
    c.wait()


def on_device(out_grads, inputs, out_basis, in_basis):
    dma = pltpu.SemaphoreType.DMA
    vm = pltpu.VMEM
    result = pl.pallas_call(
        kernel,
        out_shape=pltpu.VMEM((DO, DI), F32),
        in_specs=[pl.BlockSpec(memory_space=pl.ANY)] * 4,
        out_specs=pl.BlockSpec(memory_space=pltpu.VMEM),
        scratch_shapes=[
            vm((KO, ROWS), BF16), vm((DO, KO), BF16),
            vm((4, DO, 256), F32), vm((4, DO, 256), F32), vm((NC // 2, DO, TC), F32), vm((NC // 2, DO, TC), BF16),
            vm((NC // 2, DO, TC), BF16), vm((NC // 2, DO, TC), BF16), vm((DO, ROWS), BF16),
            vm((2, 4 * HK, 512), BF16), vm((2, 4 * HK, 512), BF16),
            vm((2, 4 * HK, WP), BF16), vm((2, 4 * HK, WQ), BF16),
            vm((NS, TS, WP), F32), vm((NS, TS, WQ), F32), vm((NS, TS, WP), RS), vm((NS, TS, WQ), RS),
            vm((NS, 3, TO, WP), RS), vm((NS, 3, TO, WQ), RS),
            vm((NS, TO, DI), F32), vm((NS, TO, DI), BF16), vm((NS, TO, DI), BF16),
            vm((ROWS, WP), BF16), vm((ROWS, WQ), BF16),
            dma((8,)), dma((4, 2)), dma((4,)), dma((4,)), dma((NC,)), dma((NC,)),
            dma((NC,)), dma((NC,)), dma((NC,)), dma((NC,)), dma((NC, 2)), dma((NC,)),
            dma((2, 3, 2)), dma((2, 3, 2)), dma((NS, 2, 3)), dma((NS, 2, 3)), dma((NS, 2)), dma((NS, 2)),
            dma((NS, 2, 3)), dma((NS, 2, 3)), dma((NS,)), dma((NS,)),
            dma((NS, 2, 3)), dma((NS, 2, 3)), dma((NS, 2, 2)), dma((NS, 2, 2)), dma((NS, 2, 2)), dma((NS, 2, 2)),
        ],
        compiler_params=pltpu.CompilerParams(
            collective_id=0, has_side_effects=True, vmem_limit_bytes=56 * 1024 * 1024
        ),
        cost_estimate=pl.CostEstimate(flops=4_600_000_000, bytes_accessed=10_600_000, transcendentals=0),
        name="correction",
    )(out_grads.T, inputs.T, out_basis.T, in_basis)
    return pl.pallas_call(
        settle,
        out_shape=jax.ShapeDtypeStruct((DO, DI), F32),
        in_specs=[pl.BlockSpec(memory_space=pltpu.VMEM)],
        out_specs=pl.BlockSpec(memory_space=pl.ANY),
        scratch_shapes=[dma],
        name="settle",
    )(pltpu.with_memory_space_constraint(result, pltpu.VMEM))


def solution(mesh):
    in_specs = (P(None, "col"), P(None, "row"), P("col", "row"), P("row", "col"))
    return jax.shard_map(
        on_device, mesh=mesh, in_specs=in_specs, out_specs=P("row", "col"), check_vma=False
    )
```

time: 83.9 us -> 65 us (0.77)
  local copies, waits for them, and re-layouts: 16.9 us -> 0 us
  Pallas kernels: 66.5 us -> 65 us
    unnamed x6 -> x0, local copies, waits for them, and re-layouts: 16.9 us -> none
    pallas_call x1 -> x2, Pallas kernels: 66.5 us -> 65 us  [the longest x1 64 us: on_device(): pl.pallas_call(kernel, out_shape=pltpu.VMEM((DO, DI), F32), in_specs=[pl....]
where the time goes in v2:
time: 65 us
  Pallas kernels  65 us (100%)
    pallas_call x1, Pallas kernels, on_device(): pl.pallas_call(kernel, out_shape=pltpu.VMEM((DO, DI), F32), in_specs=[pl....  64 us

profile of v2, /device:TPU:1, one launch (start us, length us, event | category | flops | bytes accessed | tf_op | source)
XLA Modules:
  0.0 65.0 jit_solution(8471049403598691789)
XLA Ops:
  0.0 64.0 %correction.1.src = f32[432,640]{1,0:T(8,128)S(1)} custom-call(bf16[1728,2048]{1,0:T(8,128)(2,1)} %bitcast.3, bf16[160,2048]{1,0:T(8,128)(2,1)} %bitcast.5, bf16[432,1728]{1,0:T(8,128)(2,1)} %bitcast.4, bf16[160,640]{1,0:T(8,128)(2,1)} %ib_hbm.1), custom_call_target="tpu_custom_call" | custom-call | flops 4600000000 | bytes 10600000 | tf_op jit(solution)/shard_map/correction/pallas_call | solution.py:519
  64.0 1.0 %settle.1 = f32[432,640]{1,0:T(8,128)} custom-call(f32[432,640]{1,0:T(8,128)S(1)} %correction.1.src), custom_call_target="tpu_custom_call" | custom-call | tf_op jit(solution)/shard_map/settle/pallas_call | solution.py:546

commit v3 on v2

--- a/solution.py
+++ b/solution.py
@@ -20,6 +20,7 @@
 TC = 128
 DH = 224
 NC = 2 * SEQ // TC
+STRAIGHT = range(NC - 4, NC)
 NS = 4
 TS = 512 // NS
 TO = TS // 4
@@ -29,9 +30,9 @@
 
 
 def kernel(
-    ogt_hbm, inpt_hbm, obt_hbm, ib_hbm, out_ref,
-    og, obt, po, pi, ssum, sbuf, ra, rb, orot,
-    xp, xq, bp, bq, fp, fq, sp, sq, rp, rq, gz, zs, zr, irp, irq,
+    ogt_hbm, inpt_hbm, obt_hbm, ib_hbm, orot, irp, irq,
+    og, obt, po, pi, ssum, sbuf, ra, rb,
+    xp, xq, turned, bp, bq, fp, fq, sp, sq, rp, rq, gz, zs, zr,
     ld, og_sem, core_s, core_r, coreo_s, coreo_r, za_s, za_r, zb_s, zb_r, zc_s, zc_r,
     a_s, a_r, x_s, x_r, y_s, y_r, b_s, b_r, h_s, h_r, c1_s, c1_r, c2_s, c2_r, c3_s, c3_r,
 ):
@@ -71,6 +72,7 @@
         greet(uv(0, d))
     greet(other_core)
     greet(partner)
+    greet((row, (col + 4) % 8))
 
     @pl.when(zl > 0)
     def _():
@@ -82,8 +84,6 @@
 
     ends = jnp.where((zl == 0) | (zl == 3), 1, 0)
     sends = []
-
-    pl.semaphore_wait(barrier, 10 - ends)
 
     half = pl.ds(pl.multiple_of(core * HK, 16), HK)
     axes = ((0, pu, lambda d: uv(d, 0), xp, xq, bp), (1, pv, lambda d: uv(0, d), xq, xp, bq))
@@ -147,19 +147,18 @@
 
     def load_gradients(base, jj, k):
         at = pl.ds(pl.multiple_of(base + jj * 256, 256), 256)
-        c = pltpu.make_async_copy(ogt_hbm.at[:, at], og.at[:, at], og_sem.at[jj, k])
+        c = pltpu.make_async_copy(ogt_hbm.at[:, at], og.at[k, jj], og_sem.at[jj, k])
         c.start()
         og_loads[jj, k] = c
 
-    def out_product(base, jj, k):
+    def out_product(jj, k):
         og_loads[jj, k].wait()
-        g = og[:, pl.ds(pl.multiple_of(base + jj * 256, 256), 256)]
-        return jnp.dot(obt[...], g, preferred_element_type=F32)
+        return jnp.dot(obt[...], og[k, jj], preferred_element_type=F32)
 
     core_copies = []
 
     def out_theirs(jj):
-        po[jj] = out_product(theirs, jj, 0)
+        po[jj] = out_product(jj, 0)
         c = remote(po.at[jj], pi.at[jj], core_s.at[jj], core_r.at[jj], other_core)
         c.start()
         core_copies.append(c)
@@ -169,7 +168,7 @@
         return zl if j % 2 == 0 else 3 - zl
 
     def step(j, by):
-        return (row, col + 2 * by if j % 2 == 0 else col - 2 * by)
+        return (row, (col + 2 * by) % 8 if j % 2 == 0 else (col + 8 - 2 * by) % 8)
 
     def rows(j):
         return slice(0, DH) if j % 2 == 0 else slice(DH, DO)
@@ -194,7 +193,7 @@
         return remote(piece(j), piece(j), coreo_s.at[j], coreo_r.at[j], other_core)
 
     def out_mine(jj):
-        own = out_product(mine, jj, 1)
+        own = out_product(jj, 1)
         core_copies[jj].wait_recv()
         total = own + pi[jj]
         for h in range(2):
@@ -229,6 +228,8 @@
             total = ssum[j // 2, at] + ra[j // 2, at].astype(F32) + rb[j // 2, at].astype(F32)
             piece(j)[...] = total.astype(BF16)
             zc(j, 1, 1).start()
+            if j in STRAIGHT:
+                zc(j, 2, 2).start()
             zc(j, -1, 0).start()
             co(j).start()
 
@@ -236,7 +237,8 @@
         @pl.when(role(j) == 2)
         def _():
             zc(j, 1, 0).wait_recv()
-            zc(j, 1, 0).start()
+            if j not in STRAIGHT:
+                zc(j, 1, 0).start()
             co(j).start()
 
     def out_d(j):
@@ -263,22 +265,28 @@
         @pl.when(p == 2)
         def _():
             zb(j).wait_send()
-            zc(j, 1, 0).wait_send()
+            if j not in STRAIGHT:
+                zc(j, 1, 0).wait_send()
 
         @pl.when(p == 1)
         def _():
             zc(j, -1, 0).wait_send()
             zc(j, 1, 1).wait_send()
+            if j in STRAIGHT:
+                zc(j, 2, 2).wait_send()
 
     blocks = ((0, pv, lambda d: uv(0, d), xp, bp, fp, sp, rp), (1, pu, lambda d: uv(d, 0), xq, bq, fq, sq, rq))
     b_copies = {}
 
-    def in_partial(st):
+    def in_turn(st):
         for g in range(2):
             hand[st, g].wait_recv()
         for g, pos, dev, xb, bb, f, s, r in blocks:
-            turned = xb[:, :, st * TS:(st + 1) * TS].reshape(4 * KI, TS).T
-            part = jnp.dot(turned, bb[...].reshape(4 * KI, bb.shape[-1]), preferred_element_type=F32)
+            turned[st, g] = xb[:, :, st * TS:(st + 1) * TS].reshape(4 * KI, TS).T
+
+    def in_partial(st):
+        for g, pos, dev, xb, bb, f, s, r in blocks:
+            part = jnp.dot(turned[st, g], bb[...].reshape(4 * KI, bb.shape[-1]), preferred_element_type=F32)
             f[st] = part
             s[st] = part.astype(RS)
             for i, d in enumerate(PEERS):
@@ -339,14 +347,14 @@
             for i in range(3):
                 c1[st, g, i].wait_recv()
             at = slab(buf, first, st, 0, TS)
-            for side in range(2):
-                c = remote(at, at, c2_s.at[st, g, side], c2_r.at[st, g, side], along(1 + 2 * side))
+            for side, d in enumerate(PEERS if st == NS - 1 else PEERS[:2]):
+                c = remote(at, at, c2_s.at[st, g, side], c2_r.at[st, g, side], along(d))
                 c.start()
                 c2[st, g, side] = c
                 sends.append(c)
 
     def in_forward(st):
-        for side in range(2):
+        for side in range(2) if st < NS - 1 else ():
             for g, buf, first, second, along, across in gather:
                 c2[st, g, side].wait_recv()
                 at = slab(buf, (first + 3 - 2 * side) % 4, st, side * (TS // 2), TS // 2)
@@ -357,15 +365,19 @@
 
     def in_end(st):
         for g in range(2):
-            for side in range(2):
-                c3[st, g, side].wait_recv()
-
+            if st < NS - 1:
+                for side in range(2):
+                    c3[st, g, side].wait_recv()
+            else:
+                for side in range(3):
+                    c2[st, g, side].wait_recv()
+
+    ld_ob.start()
+    load_gradients(theirs, 0, 0)
+    pl.semaphore_wait(barrier, 11 - ends)
     x_send(0)
     x_send(1)
     basis_send()
-    x_send(2)
-    ld_ob.start()
-    load_gradients(theirs, 0, 0)
     load_gradients(theirs, 1, 0)
     load_gradients(mine, 0, 1)
     load_own()
@@ -373,127 +385,138 @@
         load_gradients(mine if k else theirs, jj, k)
     ld_ob.wait()
     out_theirs(0)
+    x_send(2)
+    x_send(3)
     out_theirs(1)
-    for c in own_loads:
-        c.wait()
-    x_hand(0)
     out_mine(0)
     out_send(0)
     out_send(1)
     out_send(2)
+    out_theirs(2)
+    for c in own_loads:
+        c.wait()
+    x_hand(0)
+    x_hand(1)
     out_send(3)
     out_mine(1)
     out_send(4)
-    out_theirs(2)
     out_a(0)
+    in_turn(0)
     for c in b_blocks:
         c.wait_recv()
     in_partial(0)
+    x_hand(2)
     out_a(1)
+    in_turn(1)
     out_send(5)
-    x_hand(1)
+    out_send(6)
+    in_partial(1)
+    out_b(0)
+    out_a(2)
+    in_turn(2)
+    x_hand(3)
+    out_a(3)
+    out_a(4)
+    out_send(7)
+    in_partial(2)
+    in_cross(0)
+    in_turn(3)
+    in_partial(3)
+    in_cross(1)
     out_mine(2)
-    out_b(0)
-    x_send(3)
-    out_send(6)
-    out_a(2)
-    x_hand(2)
     out_b(1)
-    out_send(7)
-    out_a(3)
-    in_partial(1)
-    in_cross(0)
+    out_b(2)
+    out_a(5)
     out_send(8)
-    out_a(4)
-    in_partial(2)
-    x_hand(3)
     out_c(0)
-    out_b(2)
-    out_c(1)
-    in_cross(1)
+    out_send(9)
     out_b(3)
-    out_a(5)
-    out_send(9)
     out_a(6)
-    in_partial(3)
-    out_c(2)
-    out_a(7)
     out_b(4)
     in_cross(2)
     out_send(10)
     out_theirs(3)
+    out_a(7)
+    out_send(11)
+    in_cross(3)
+    out_c(1)
     out_a(8)
-    out_send(11)
+    out_a(9)
+    out_b(5)
     in_round(0)
-    in_cross(3)
-    out_b(5)
+    out_mine(3)
+    out_c(2)
+    out_b(6)
+    out_send(12)
+    out_send(13)
     out_c(3)
-    out_mine(3)
-    out_b(6)
+    out_send(14)
+    out_d(0)
+    out_c(4)
+    out_a(10)
     in_round(1)
     out_b(7)
-    out_d(0)
-    out_send(12)
     in_spread(0)
-    out_a(9)
-    out_a(10)
+    out_a(11)
+    out_send(15)
     out_b(8)
+    in_round(2)
+    out_a(12)
+    out_c(5)
+    in_round(3)
     out_d(1)
-    in_round(2)
     in_spread(1)
-    out_c(4)
-    out_c(5)
-    out_a(11)
+    out_b(9)
     out_d(2)
-    in_round(3)
+    out_d(3)
+    out_d(4)
+    out_a(13)
+    in_forward(0)
     out_c(6)
-    out_send(13)
-    out_d(3)
+    out_b(10)
+    out_a(14)
+    out_c(7)
+    out_a(15)
+    out_b(11)
     in_spread(2)
-    out_send(14)
-    out_send(15)
-    out_c(7)
-    in_forward(0)
-    out_b(9)
+    out_b(12)
     out_c(8)
-    out_a(12)
-    out_b(10)
-    out_d(4)
-    out_b(11)
+    in_spread(3)
+    out_b(13)
     out_d(5)
-    out_a(13)
+    out_c(9)
+    in_forward(1)
     out_d(6)
+    out_c(10)
     out_d(7)
-    in_spread(3)
-    out_c(9)
-    out_a(14)
-    out_c(10)
-    out_a(15)
-    in_forward(1)
-    out_d(8)
-    out_b(12)
+    out_b(14)
+    out_b(15)
     in_forward(2)
     out_c(11)
-    out_b(13)
+    out_d(8)
+    out_d(9)
+    out_c(12)
+    out_c(13)
     in_forward(3)
-    out_b(14)
-    out_b(15)
-    out_d(9)
     out_d(10)
-    out_c(12)
     out_d(11)
     out_d(12)
     out_d(13)
-    out_c(13)
+    out_d(14)
     out_c(14)
-    out_d(14)
+    out_d(15)
     out_c(15)
-    out_d(15)
     for j in range(NC):
         out_end(j)
     for st in range(NS):
         in_end(st)
 
+    for c in sends:
+        c.wait_send()
+
+
+def correct(orot, irp, irq, out_hbm, held, sem):
+    stores = []
     for m in range(3):
         part = slice(m * 144, (m + 1) * 144)
         for lanes, ir in ((slice(0, WP), irp), (slice(WP, DI), irq)):
@@ -502,15 +525,12 @@
                 seq = slice(n * SEQ, (n + 1) * SEQ)
                 prod = jnp.dot(orot[part, seq], ir[seq, :], preferred_element_type=F32)
                 acc = prod * prod if acc is None else acc + prod * prod
-            out_ref[part, lanes] = acc * F32(1.0 / ROWS)
-    for c in sends:
-        c.wait_send()
-
-
-def settle(src, dst, go):
-    c = pltpu.make_async_copy(src, dst, go)
-    c.start()
-    c.wait()
+            held[part, lanes] = acc * F32(1.0 / ROWS)
+        c = pltpu.make_async_copy(held.at[part], out_hbm.at[part], sem.at[m])
+        c.start()
+        stores.append(c)
+    for c in stores:
+        c.wait()
 
 
 def on_device(out_grads, inputs, out_basis, in_basis):
@@ -518,24 +538,23 @@
     vm = pltpu.VMEM
     result = pl.pallas_call(
         kernel,
-        out_shape=pltpu.VMEM((DO, DI), F32),
+        out_shape=(vm((DO, ROWS), BF16), vm((ROWS, WP), BF16), vm((ROWS, WQ), BF16)),
         in_specs=[pl.BlockSpec(memory_space=pl.ANY)] * 4,
-        out_specs=pl.BlockSpec(memory_space=pltpu.VMEM),
+        out_specs=[pl.BlockSpec(memory_space=pltpu.VMEM)] * 3,
         scratch_shapes=[
-            vm((KO, ROWS), BF16), vm((DO, KO), BF16),
+            vm((2, 4, KO, 256), BF16), vm((DO, KO), BF16),
             vm((4, DO, 256), F32), vm((4, DO, 256), F32), vm((NC // 2, DO, TC), F32), vm((NC // 2, DO, TC), BF16),
-            vm((NC // 2, DO, TC), BF16), vm((NC // 2, DO, TC), BF16), vm((DO, ROWS), BF16),
-            vm((2, 4 * HK, 512), BF16), vm((2, 4 * HK, 512), BF16),
+            vm((NC // 2, DO, TC), BF16), vm((NC // 2, DO, TC), BF16),
+            vm((2, 4 * HK, 512), BF16), vm((2, 4 * HK, 512), BF16), vm((NS, 2, TS, 4 * KI), BF16),
             vm((2, 4 * HK, WP), BF16), vm((2, 4 * HK, WQ), BF16),
             vm((NS, TS, WP), F32), vm((NS, TS, WQ), F32), vm((NS, TS, WP), RS), vm((NS, TS, WQ), RS),
             vm((NS, 3, TO, WP), RS), vm((NS, 3, TO, WQ), RS),
             vm((NS, TO, DI), F32), vm((NS, TO, DI), BF16), vm((NS, TO, DI), BF16),
-            vm((ROWS, WP), BF16), vm((ROWS, WQ), BF16),
             dma((8,)), dma((4, 2)), dma((4,)), dma((4,)), dma((NC,)), dma((NC,)),
-            dma((NC,)), dma((NC,)), dma((NC,)), dma((NC,)), dma((NC, 2)), dma((NC,)),
+            dma((NC,)), dma((NC,)), dma((NC,)), dma((NC,)), dma((NC, 3)), dma((NC,)),
             dma((2, 3, 2)), dma((2, 3, 2)), dma((NS, 2, 3)), dma((NS, 2, 3)), dma((NS, 2)), dma((NS, 2)),
             dma((NS, 2, 3)), dma((NS, 2, 3)), dma((NS,)), dma((NS,)),
-            dma((NS, 2, 3)), dma((NS, 2, 3)), dma((NS, 2, 2)), dma((NS, 2, 2)), dma((NS, 2, 2)), dma((NS, 2, 2)),
+            dma((NS, 2, 3)), dma((NS, 2, 3)), dma((NS, 2, 3)), dma((NS, 2, 3)), dma((NS, 2, 2)), dma((NS, 2, 2)),
         ],
         compiler_params=pltpu.CompilerParams(
             collective_id=0, has_side_effects=True, vmem_limit_bytes=56 * 1024 * 1024
@@ -544,13 +563,14 @@
         name="correction",
     )(out_grads.T, inputs.T, out_basis.T, in_basis)
     return pl.pallas_call(
-        settle,
+        correct,
         out_shape=jax.ShapeDtypeStruct((DO, DI), F32),
-        in_specs=[pl.BlockSpec(memory_space=pltpu.VMEM)],
+        in_specs=[pl.BlockSpec(memory_space=pltpu.VMEM)] * 3,
         out_specs=pl.BlockSpec(memory_space=pl.ANY),
-        scratch_shapes=[dma],
-        name="settle",
-    )(pltpu.with_memory_space_constraint(result, pltpu.VMEM))
+        scratch_shapes=[vm((DO, DI), F32), dma((3,))],
+        compiler_params=pltpu.CompilerParams(vmem_limit_bytes=48 * 1024 * 1024),
+        name="correct",
+    )(*(pltpu.with_memory_space_constraint(r, pltpu.VMEM) for r in result))
 
 
 def solution(mesh):

time: 65 us -> 60.1 us (0.925)
  Pallas kernels: 65 us -> 60 us
    pallas_call x2, Pallas kernels: 65 us -> 60 us  [the longest x1 57.7 us: on_device(): pl.pallas_call(kernel, out_shape=(vm((DO, ROWS), BF16), vm((ROWS, WP), BF...]
where the time goes in v3:
time: 60.1 us
  Pallas kernels  60 us (100%)
    pallas_call x1, Pallas kernels, on_device(): pl.pallas_call(kernel, out_shape=(vm((DO, ROWS), BF16), vm((ROWS, WP), BF...  57.7 us
    pallas_call x1, Pallas kernels, on_device(): pl.pallas_call(correct, out_shape=jax.ShapeDtypeStruct((DO, DI), F32), in...  2.31 us

profile of v3, /device:TPU:1, one launch (start us, length us, event | category | flops | bytes accessed | tf_op | source)
XLA Modules:
  0.0 60.1 jit_solution(9695212138881028207)
XLA Ops:
  0.0 57.7 %correction.1 = (bf16[432,2048]{1,0:T(8,128)(2,1)S(1)}, bf16[2048,384]{1,0:T(8,128)(2,1)S(1)}, bf16[2048,256]{1,0:T(8,128)(2,1)S(1)}) custom-call(bf16[1728,2048]{1,0:T(8,128)(2,1)} %bitcast.3, bf16[160,2048]{1,0:T(8,128)(2,1)} %bitcast.5, bf16[432,1728]{1,0:T(8,128)(2,1)} %bitcast.4, bf16[160,640]{1,0:T(8,128)(2,1)} %ib_hbm.1), custom_call_target="tpu_custom_call" | custom-call | flops 4600000000 | bytes 10600000 | tf_op jit(solution)/shard_map/correction/pallas_call | solution.py:539
  57.7 2.3 %correct.1 = f32[432,640]{1,0:T(8,128)} custom-call(bf16[432,2048]{1,0:T(8,128)(2,1)S(1)} %get-tuple-element.8.orot, bf16[2048,384]{1,0:T(8,128)(2,1)S(1)} %get-tuple-element.9.irp, bf16[2048,256]{1,0:T(8,128)(2,1)S(1)} %get-tuple-element.10.irq), custom_call_target="tpu_custom_call" | custom-call | tf_op jit(solution)/shard_map/correct/pallas_call | solution.py:565

commit v4 on v3

--- a/solution.py
+++ b/solution.py
@@ -376,7 +376,6 @@
     load_gradients(theirs, 0, 0)
     pl.semaphore_wait(barrier, 11 - ends)
     x_send(0)
-    x_send(1)
     basis_send()
     load_gradients(theirs, 1, 0)
     load_gradients(mine, 0, 1)
@@ -385,127 +384,128 @@
         load_gradients(mine if k else theirs, jj, k)
     ld_ob.wait()
     out_theirs(0)
+    x_send(1)
+    out_theirs(1)
     x_send(2)
-    x_send(3)
-    out_theirs(1)
     out_mine(0)
     out_send(0)
     out_send(1)
-    out_send(2)
-    out_theirs(2)
     for c in own_loads:
         c.wait()
     x_hand(0)
-    x_hand(1)
+    out_send(2)
     out_send(3)
+    out_theirs(2)
     out_mine(1)
+    in_turn(0)
+    out_a(0)
     out_send(4)
-    out_a(0)
-    in_turn(0)
+    x_send(3)
     for c in b_blocks:
         c.wait_recv()
     in_partial(0)
-    x_hand(2)
-    out_a(1)
-    in_turn(1)
     out_send(5)
     out_send(6)
+    out_a(1)
+    x_hand(1)
+    out_mine(2)
+    out_a(2)
+    out_a(3)
+    out_b(0)
+    x_hand(2)
+    out_send(7)
+    in_turn(1)
+    out_send(8)
+    out_a(4)
     in_partial(1)
-    out_b(0)
-    out_a(2)
+    x_hand(3)
+    out_b(1)
+    in_cross(0)
+    out_send(9)
+    out_a(5)
     in_turn(2)
-    x_hand(3)
-    out_a(3)
-    out_a(4)
-    out_send(7)
     in_partial(2)
-    in_cross(0)
+    out_a(6)
+    out_b(2)
+    out_b(3)
     in_turn(3)
     in_partial(3)
     in_cross(1)
-    out_mine(2)
-    out_b(1)
-    out_b(2)
-    out_a(5)
-    out_send(8)
     out_c(0)
-    out_send(9)
-    out_b(3)
-    out_a(6)
     out_b(4)
+    out_a(7)
     in_cross(2)
     out_send(10)
+    out_a(8)
+    out_send(11)
     out_theirs(3)
-    out_a(7)
-    out_send(11)
+    out_c(1)
     in_cross(3)
-    out_c(1)
-    out_a(8)
+    out_mine(3)
+    out_b(5)
+    out_d(0)
+    out_send(12)
+    in_round(0)
+    out_b(6)
+    out_send(13)
+    out_c(2)
     out_a(9)
-    out_b(5)
-    in_round(0)
-    out_mine(3)
-    out_c(2)
-    out_b(6)
-    out_send(12)
-    out_send(13)
+    out_a(10)
+    out_send(14)
+    in_round(1)
     out_c(3)
-    out_send(14)
-    out_d(0)
+    out_b(7)
     out_c(4)
-    out_a(10)
-    in_round(1)
-    out_b(7)
+    out_d(1)
     in_spread(0)
+    out_d(2)
     out_a(11)
     out_send(15)
+    out_a(12)
     out_b(8)
     in_round(2)
-    out_a(12)
+    out_b(9)
+    out_a(13)
+    in_round(3)
     out_c(5)
-    in_round(3)
-    out_d(1)
+    out_b(10)
+    out_c(6)
     in_spread(1)
-    out_b(9)
-    out_d(2)
+    out_a(14)
     out_d(3)
-    out_d(4)
-    out_a(13)
-    in_forward(0)
-    out_c(6)
-    out_b(10)
-    out_a(14)
+    out_b(11)
     out_c(7)
     out_a(15)
-    out_b(11)
+    out_b(12)
+    in_forward(0)
+    out_d(4)
+    out_b(13)
     in_spread(2)
-    out_b(12)
     out_c(8)
+    out_c(9)
+    out_d(5)
+    out_d(6)
     in_spread(3)
-    out_b(13)
-    out_d(5)
-    out_c(9)
+    out_b(14)
+    out_c(10)
+    out_c(11)
+    out_d(7)
+    out_b(15)
     in_forward(1)
-    out_d(6)
-    out_c(10)
-    out_d(7)
-    out_b(14)
-    out_b(15)
+    out_d(8)
     in_forward(2)
-    out_c(11)
-    out_d(8)
     out_d(9)
     out_c(12)
-    out_c(13)
-    in_forward(3)
     out_d(10)
     out_d(11)
+    out_c(13)
     out_d(12)
     out_d(13)
     out_d(14)
+    out_d(15)
     out_c(14)
-    out_d(15)
     out_c(15)
+    in_forward(3)
     for j in range(NC):
         out_end(j)
     for st in range(NS):

time: 60.1 us -> 58.3 us (0.970)
  Pallas kernels: 60 us -> 58.2 us
    pallas_call x1, Pallas kernels: 57.7 us -> 55.9 us  [on_device(): pl.pallas_call(kernel, out_shape=(vm((DO, ROWS), BF16), vm((ROWS, WP), BF...]
where the time goes in v4:
time: 58.3 us; the launch traced here: 58.2 us
  Pallas kernels  58.2 us (100%)
    pallas_call x1, Pallas kernels, on_device(): pl.pallas_call(kernel, out_shape=(vm((DO, ROWS), BF16), vm((ROWS, WP), BF...  55.9 us
    pallas_call x1, Pallas kernels, on_device(): pl.pallas_call(correct, out_shape=jax.ShapeDtypeStruct((DO, DI), F32), in...  2.31 us

profile of v4, /device:TPU:1, one launch (start us, length us, event | category | flops | bytes accessed | tf_op | source)
XLA Modules:
  0.0 58.2 jit_solution(14607843259469320186)
XLA Ops:
  0.0 55.9 %correction.1 = (bf16[432,2048]{1,0:T(8,128)(2,1)S(1)}, bf16[2048,384]{1,0:T(8,128)(2,1)S(1)}, bf16[2048,256]{1,0:T(8,128)(2,1)S(1)}) custom-call(bf16[1728,2048]{1,0:T(8,128)(2,1)} %bitcast.3, bf16[160,2048]{1,0:T(8,128)(2,1)} %bitcast.5, bf16[432,1728]{1,0:T(8,128)(2,1)} %bitcast.4, bf16[160,640]{1,0:T(8,128)(2,1)} %ib_hbm.1), custom_call_target="tpu_custom_call" | custom-call | flops 4600000000 | bytes 10600000 | tf_op jit(solution)/shard_map/correction/pallas_call | solution.py:539
  55.9 2.3 %correct.1 = f32[432,640]{1,0:T(8,128)} custom-call(bf16[432,2048]{1,0:T(8,128)(2,1)S(1)} %get-tuple-element.8.orot, bf16[2048,384]{1,0:T(8,128)(2,1)S(1)} %get-tuple-element.9.irp, bf16[2048,256]{1,0:T(8,128)(2,1)S(1)} %get-tuple-element.10.irq), custom_call_target="tpu_custom_call" | custom-call | tf_op jit(solution)/shard_map/correct/pallas_call | solution.py:565

commit v5 on v4

--- a/solution.py
+++ b/solution.py
@@ -20,7 +20,7 @@
 TC = 128
 DH = 224
 NC = 2 * SEQ // TC
-STRAIGHT = range(NC - 4, NC)
+STRAIGHT = range(NC - 6, NC)
 NS = 4
 TS = 512 // NS
 TO = TS // 4

time: 58.3 us -> 58.2 us (level)
  no operation moved by 1% of the time
where the time goes in v5:
time: 58.2 us; the launch traced here: 58.1 us
  Pallas kernels  58.1 us (100%)
    pallas_call x1, Pallas kernels, on_device(): pl.pallas_call(kernel, out_shape=(vm((DO, ROWS), BF16), vm((ROWS, WP), BF...  55.8 us
    pallas_call x1, Pallas kernels, on_device(): pl.pallas_call(correct, out_shape=jax.ShapeDtypeStruct((DO, DI), F32), in...  2.31 us

profile of v5, /device:TPU:1, one launch (start us, length us, event | category | flops | bytes accessed | tf_op | source)
XLA Modules:
  0.0 58.1 jit_solution(9330216771972685920)
XLA Ops:
  0.0 55.8 %correction.1 = (bf16[432,2048]{1,0:T(8,128)(2,1)S(1)}, bf16[2048,384]{1,0:T(8,128)(2,1)S(1)}, bf16[2048,256]{1,0:T(8,128)(2,1)S(1)}) custom-call(bf16[1728,2048]{1,0:T(8,128)(2,1)} %bitcast.3, bf16[160,2048]{1,0:T(8,128)(2,1)} %bitcast.5, bf16[432,1728]{1,0:T(8,128)(2,1)} %bitcast.4, bf16[160,640]{1,0:T(8,128)(2,1)} %ib_hbm.1), custom_call_target="tpu_custom_call" | custom-call | flops 4600000000 | bytes 10600000 | tf_op jit(solution)/shard_map/correction/pallas_call | solution.py:539
  55.8 2.3 %correct.1 = f32[432,640]{1,0:T(8,128)} custom-call(bf16[432,2048]{1,0:T(8,128)(2,1)S(1)} %get-tuple-element.8.orot, bf16[2048,384]{1,0:T(8,128)(2,1)S(1)} %get-tuple-element.9.irp, bf16[2048,256]{1,0:T(8,128)(2,1)S(1)} %get-tuple-element.10.irq), custom_call_target="tpu_custom_call" | custom-call | tf_op jit(solution)/shard_map/correct/pallas_call | solution.py:565
